TPU v7x, 32 devices: a whole 2x2x4 slice. The times are simulated.
32 devices in a mesh: row: 4 (over y, x), col: 8 (over z, core).
Axes of the slice: x: 2, y: 2, z: 4, core: 2. Of those that a mesh axis runs over, the one named last changes fastest.
Arguments:
- ancestor_inverse: float32 [4096, 4096], P('row', 'col'), may hold values from -18 to 18, as said below
- panel: float32 [4096, 1024], P(('row', 'col')), may hold values from -0.09375 to 0.09375
- diag_inverse: float32 [1024, 1024], replicated, may hold values from -0.1875 to 0.1875
- inverse_pattern: int32 [16, 16], replicated, may hold values from 0 to 1, as said below
- panel_pattern: int32 [16, 4], replicated, may hold values 0 or 1
Outputs:
- sigma_panel: float32 [4096, 1024], P(('row', 'col'))
- sigma_diag: float32 [1024, 1024], replicated
Inputs may be any that keep to these rules, and one draw needn't show every extreme that they name: `ancestor_inverse`: symmetric, so entry (i, j) equals entry (j, i). `inverse_pattern`: 1 marks a kept tile; the pattern is symmetric and every diagonal tile is kept. `panel_pattern`: 1 marks a nonzero tile.
All inputs are finite; a program needn't handle non-finite values.
Results may differ from a plain program's by a relative error of at most 0.000075.
Values sent between devices are 32-bit elements; how exact they have to be, the bound alone decides.
A program may use at most 128 MiB of HBM per device.

v0:
```python
import jax
import jax.numpy as jnp
from jax import lax
from jax.sharding import PartitionSpec as P

TILE = 256


HIGH = lax.Precision.HIGHEST


def from_root(value, axis, source):
    kept = jnp.where(lax.axis_index(axis) == source, value, 0).astype(value.dtype)
    return lax.psum(kept, axis)


def shards(ancestor_inverse, panel, diag_inverse, inverse_pattern, panel_pattern):
    rows_count = lax.axis_size("row")
    cols_count = lax.axis_size("col")
    row_at = lax.axis_index("row")
    col_at = lax.axis_index("col")
    block_rows, block_cols = ancestor_inverse.shape
    piece_rows, panel_width = panel.shape
    inv_factor = jnp.tril(diag_inverse) + jnp.eye(panel_width, dtype=jnp.float32)
    first_row = (row_at * cols_count + col_at) * piece_rows
    tile_ids = (first_row + jnp.arange(piece_rows, dtype=jnp.int32)) // TILE
    one_hot = (
        tile_ids[:, None] == jnp.arange(panel_pattern.shape[0], dtype=jnp.int32)[None, :]
    ).astype(jnp.float32)
    row_flags = jnp.dot(one_hot, panel_pattern.astype(jnp.float32), precision=HIGH)
    local_scaled = jnp.dot(panel * jnp.repeat(row_flags, TILE, axis=1), inv_factor, precision=HIGH)
    row_band = lax.all_gather(local_scaled, "col", axis=0, tiled=True)
    col_ratio = cols_count // rows_count
    root_row = col_at // col_ratio
    broadcast_band = from_root(row_band, "row", root_row)
    col_scaled = lax.dynamic_slice_in_dim(
        broadcast_band, col_at % col_ratio * block_cols, block_cols, 0
    )
    row_tiles = block_rows // TILE
    col_tiles = block_cols // TILE
    tile_flags = lax.dynamic_slice(
        inverse_pattern, (row_at * row_tiles, col_at * col_tiles), (row_tiles, col_tiles)
    )
    flag_values = tile_flags.astype(jnp.float32)
    masked_inverse = (
        ancestor_inverse.reshape(row_tiles, TILE, col_tiles, TILE) * flag_values[:, None, :, None]
    ).reshape(block_rows, block_cols)
    sigma_panel = lax.psum_scatter(
        -jnp.dot(masked_inverse, col_scaled, precision=HIGH), "col", scatter_dimension=0, tiled=True
    )
    quad_form = jnp.einsum("rj,rk->jk", local_scaled, sigma_panel, precision=HIGH)
    base_term = jnp.einsum("kj,kl->jl", inv_factor, inv_factor, precision=HIGH)
    local_term = -quad_form
    summed_term = lax.psum(local_term, ("row", "col"))
    sigma_diag = base_term + summed_term
    return (sigma_panel, sigma_diag)


def solution(mesh):
    return jax.shard_map(
        shards,
        mesh=mesh,
        in_specs=(P("row", "col"), P(("row", "col"), None), P(), P(), P()),
        out_specs=(P(("row", "col"), None), P()),
        check_vma=False,
    )
```

profile of v0, /device:TPU:0, one launch (start us, length us, event | category | flops | bytes accessed | tf_op | source)
XLA Modules:
  0.0 404.2 jit_solution(6052688358625914567)
XLA Ops:
  7.2 0.0 all-gather.2.cloned.1.call-start
  7.2 0.9 fusion.8
  8.2 0.2 broadcast_in_dim.12
  8.4 0.1 copy.10
  8.5 5.3 %fusion.1 = f32[128,1024]{1,0:T(8,128)} fusion(f32[1024,1024]{1,0:T(8,128)} %param.7, f32[128,1024]{1,0:T(8,128)} %param.6, f32[128,1024]{1,0:T(8,128)S(1)} %bitcast.10), kind=kOutput, calls=%fused_computation.4 | convolution fusion | flops 1615986688 | bytes 5767168 | tf_op jit(solution)/shard_map/dot_general | solution.py:31
  13.7 0.0 all-gather.2.cloned.1.call-update
  13.8 0.0 all-reduce.3.cloned.1.call-start
  13.8 49.9 %all-gather.2.cloned.1.call-done = f32[1024,1024]{1,0:T(8,128)} async-done(((f32[128,1024]{1,0:T(8,128)}), f32[1024,1024]{1,0:T(8,128)}) %all-gather.2.cloned.1.call-update) | async-done | bytes 4194320 | tf_op jit(solution)/shard_map/all_gather | solution.py:32
  63.8 5.0 %broadcast_select_fusion = f32[1024,1024]{1,0:T(8,128)} fusion(f32[1024,1024]{1,0:T(8,128)} %all-gather.2.cloned.1.call-done, pred[]{:T(512)S(6)} %eq.21), kind=kLoop, calls=%fused_computation.9 | loop fusion | flops 1048576 | bytes 8388609 | tf_op jit(solution)/shard_map/jit(_where)/select_n | solution.py:13
  68.8 0.0 all-reduce.3.cloned.1.call-update
  68.8 0.0 reduce-scatter.2.cloned.1.call-start
  68.9 0.8 dynamic-slice_convert_fusion
  69.7 0.6 mul.31
  70.3 0.2 copy.9
  70.5 101.1 %all-reduce.3.cloned.1.call-done = f32[1024,1024]{1,0:T(8,128)} async-done(((f32[1024,1024]{1,0:T(8,128)}), f32[1024,1024]{1,0:T(8,128)}) %all-reduce.3.cloned.1.call-update) | async-done | bytes 4194320 | tf_op jit(solution)/shard_map/psum | solution.py:14
  171.5 10.2 %convolution_negate_fusion.1 = f32[1024,1024]{1,0:T(8,128)} fusion(f32[1024,1024]{1,0:T(8,128)} %all-reduce.3.cloned.1.call-done, s32[]{:T(128)S(6)} %select_n.49, f32[1024,512]{1,0:T(8,128)} %param.5, f32[1024,512]{1,0:T(8,128)S(1)} %bitcast.7), kind=kOutput, calls=%fused_computation.6 | convolution fusion | flops 6444023808 | bytes 10485764 | tf_op jit(solution)/shard_map/dot_general | solution.py:49
  181.7 0.0 copy-start
  181.7 0.0 reduce-scatter.2.cloned.1.call-update
  181.7 0.2 all-reduce.5.cloned.1.call-start
  181.9 49.9 %reduce-scatter.2.cloned.1.call-done = f32[128,1024]{1,0:T(8,128)} async-done(((f32[1024,1024]{1,0:T(8,128)}), f32[128,1024]{1,0:T(8,128)}) %reduce-scatter.2.cloned.1.call-update) | async-done | bytes 524304 | tf_op jit(solution)/shard_map/reduce_scatter | solution.py:48
  231.9 0.0 copy-done
  231.9 6.0 %convolution_negate_fusion = f32[1024,1024]{1,0:T(8,128)} fusion(f32[128,1024]{1,0:T(8,128)S(1)} %copy-done, f32[128,1024]{1,0:T(8,128)} %reduce-scatter.2.cloned.1.call-done), kind=kOutput, calls=%fused_computation.5 | convolution fusion | flops 1611661312 | bytes 5242880 | tf_op jit(solution)/shard_map/rj,rk->jk/dot_general | solution.py:51
  237.9 0.0 all-reduce.5.cloned.1.call-update
  237.9 140.7 %all-reduce.5.cloned.1.call-done = f32[1024,1024]{1,0:T(8,128)} async-done(((f32[1024,1024]{1,0:T(8,128)}), f32[1024,1024]{1,0:T(8,128)}) %all-reduce.5.cloned.1.call-update) | async-done | bytes 4194320 | tf_op jit(solution)/shard_map/psum | solution.py:54
  378.6 19.0 %fusion.6 = f32[1024,1024]{1,0:T(8,128)} fusion(f32[1024,1024]{1,0:T(8,128)} %all-reduce.5.cloned.1.call-done, f32[1024,1024]{1,0:T(8,128)} %param.7), kind=kOutput, calls=%fused_computation.12 | convolution fusion | flops 12891193344 | bytes 12582912 | tf_op jit(solution)/shard_map/kj,kl->jl/dot_general | solution.py:52
  (1 shorter events, 0.0 us)
Async XLA Ops:
  7.2 56.6 %all-gather.2.cloned.1.call-start = ((), (), s32[]{:S(2)}) async-start(), calls=%async_computation.1 | async-start | bytes 4718592 | tf_op jit(solution)/shard_map/all_gather | solution.py:32
  13.8 157.8 %all-reduce.3.cloned.1.call-start = ((), (), s32[]{:S(2)}) async-start(), calls=%async_computation.2 | async-start | bytes 8388608 | tf_op jit(solution)/shard_map/psum | solution.py:14
  68.8 163.1 %reduce-scatter.2.cloned.1.call-start = ((), (), s32[]{:S(2)}) async-start(), calls=%async_computation.3 | async-start | bytes 4718592 | tf_op jit(solution)/shard_map/reduce_scatter | solution.py:48
  181.7 50.2 %copy-start = (f32[128,1024]{1,0:T(8,128)S(1)}, f32[128,1024]{1,0:T(8,128)}, u32[]{:S(2)}) copy-start(f32[128,1024]{1,0:T(8,128)} %fusion.1) | copy-start | bytes 1572868
  181.7 196.9 %all-reduce.5.cloned.1.call-start = ((), (), s32[]{:S(2)}) async-start(), calls=%async_computation.4 | async-start | bytes 8388608 | tf_op jit(solution)/shard_map/psum | solution.py:54
Sparse Core Ops, SparseCore 0:
  13.9 49.8 all-gather.1
  68.9 102.5 all-reduce.2
  181.8 49.9 reduce-scatter.1
  238.8 139.7 all-reduce.4
where the time goes:
time: 404 us
  waiting for transfers between devices  342 us (85%)
  matrix products  41.4 us (10%)
  between operations  13.9 us (3%)
  other arithmetic  5.8 us (1%)
    psum x1, waiting for transfers between devices, shards(): summed_term = lax.psum(local_term, ('row', 'col'))  141 us
    psum x1, waiting for transfers between devices, from_root(): return lax.psum(kept, axis)  101 us
    all_gather x1, waiting for transfers between devices, shards(): row_band = lax.all_gather(local_scaled, 'col', axis=0, tiled=True)  49.9 us
    reduce_scatter x1, waiting for transfers between devices, shards(): lax.psum_scatter(-jnp.dot(masked_inverse, col_scaled, precision=HIGH), 'c...  49.9 us
    dot_general x1, matrix products, shards(): base_term = jnp.einsum('kj,kl->jl', inv_factor, inv_factor, precision=HIGH)  19 us
    dot_general x1, matrix products, shards(): jnp.dot(masked_inverse, col_scaled, precision=HIGH)  10.2 us
  transfers between devices with their start and end apart: 4, of which 4 were waited for; matrix products, arithmetic and copies ran while one was open for 0% of the time, Pallas kernels for 0%

commit v1 on v0

v1 whole, which is shorter than its diff:
```python
import jax
import jax.numpy as jnp
from jax import lax
from jax.sharding import PartitionSpec as P

TILE = 256


HIGH = lax.Precision.HIGH


def shards(ancestor_inverse, panel, diag_inverse, inverse_pattern, panel_pattern):
    rows_count = lax.axis_size("row")
    cols_count = lax.axis_size("col")
    row_at = lax.axis_index("row")
    col_at = lax.axis_index("col")
    block_rows, block_cols = ancestor_inverse.shape
    piece_rows, panel_width = panel.shape
    place = row_at * cols_count + col_at
    inv_factor = jnp.tril(diag_inverse) + jnp.eye(panel_width, dtype=jnp.float32)
    row_flags = lax.dynamic_slice_in_dim(panel_pattern, place * piece_rows // TILE, 1, 0).astype(jnp.float32)
    local_scaled = jnp.dot(panel * jnp.repeat(row_flags, TILE, axis=1), inv_factor, precision=HIGH)
    row_band = lax.all_gather(local_scaled, "col", axis=0, tiled=True)
    row_tiles = block_rows // TILE
    col_tiles = block_cols // TILE
    tile_flags = lax.dynamic_slice(
        inverse_pattern, (row_at * row_tiles, col_at * col_tiles), (row_tiles, col_tiles)
    )
    flag_values = tile_flags.astype(jnp.float32)
    masked_inverse = (
        ancestor_inverse.reshape(row_tiles, TILE, col_tiles, TILE) * flag_values[:, None, :, None]
    ).reshape(block_rows, block_cols)
    partial = -lax.dot_general(masked_inverse, row_band, (((0,), (0,)), ((), ())), precision=HIGH)
    summed = lax.psum_scatter(partial, "row", scatter_dimension=0, tiled=True)
    moves = [(r * cols_count + c, c * rows_count + r) for r in range(rows_count) for c in range(cols_count)]
    sigma_panel = lax.ppermute(summed, ("row", "col"), moves)
    share = panel_width // (rows_count * cols_count)
    factor_rows = lax.dynamic_slice_in_dim(inv_factor, place * share, share, 0)
    left = jnp.concatenate([local_scaled, factor_rows], axis=0)
    right = jnp.concatenate([-sigma_panel, factor_rows], axis=0)
    bands = []
    count = panel_width // TILE
    for i in range(count):
        part = lax.dot_general(
            left[:, i * TILE : (i + 1) * TILE], right[:, : (i + 1) * TILE], (((0,), (0,)), ((), ())), precision=HIGH
        )
        bands += [part[:, j * TILE : (j + 1) * TILE] for j in range(i + 1)]
    summed_tiles = lax.psum(jnp.concatenate(bands, axis=0), ("row", "col"))
    tile_at = lambda i, j: summed_tiles[(i * (i + 1) // 2 + j) * TILE :][:TILE]
    sigma_diag = jnp.concatenate(
        [
            jnp.concatenate([tile_at(i, j) if i >= j else tile_at(j, i).T for j in range(count)], axis=1)
            for i in range(count)
        ],
        axis=0,
    )
    return (sigma_panel, sigma_diag)


def solution(mesh):
    return jax.shard_map(
        shards,
        mesh=mesh,
        in_specs=(P("row", "col"), P(("row", "col"), None), P(), P(), P()),
        out_specs=(P(("row", "col"), None), P()),
        check_vma=False,
    )
```

time: 404 us -> 284 us (0.70)
  waiting for transfers between devices: 342 us -> 236 us
  matrix products: 41.4 us -> 14.1 us
  local copies, waits for them, and re-layouts: 1.08 us -> 7.16 us
  other arithmetic: 5.8 us -> 10.3 us
    psum x2 -> x1, waiting for transfers between devices: 242 us -> 154 us  [shards(): summed_tiles = lax.psum(jnp.concatenate(bands, axis=0), ('row', 'col'))]
    dot_general x4 -> x5, matrix products: 36.1 us -> 9.76 us  [the longest x1 7.71 us: shards(): lax.dot_general(masked_inverse, row_band, (((0,), (0,)), ((), ())), preci...]
    reduce_scatter x1, waiting for transfers between devices: 49.9 us -> 34 us  [shards(): summed = lax.psum_scatter(partial, 'row', scatter_dimension=0, tiled=True)]
    concatenate x0 -> x2, other arithmetic: none -> 5.93 us  [the longest x1 5.86 us: shards(): jnp.concatenate([jnp.concatenate([tile_at(i, j) if i >= j else tile_at(j,...]
    select_n x2 -> x0, other arithmetic: 5.04 us -> none  [the longest x1 5.03 us: from_root(): jnp.where(lax.axis_index(axis) == source, value, 0).astype(value.dtype)]
  transfers between devices with their start and end apart: 4 -> 4, of which waited for: 4 -> 3; matrix products, arithmetic and copies ran while one was open for 0% -> 2% of each run, Pallas kernels for 0% -> 0%
where the time goes in v1:
time: 284 us
  waiting for transfers between devices  236 us (83%)
  matrix products  14.1 us (5%)
  between operations  14 us (5%)
  other arithmetic  10.3 us (4%)
  local copies, waits for them, and re-layouts  7.16 us (3%)
    psum x1, waiting for transfers between devices, shards(): summed_tiles = lax.psum(jnp.concatenate(bands, axis=0), ('row', 'col'))  154 us
    all_gather x1, waiting for transfers between devices, shards(): row_band = lax.all_gather(local_scaled, 'col', axis=0, tiled=True)  48.4 us
    reduce_scatter x1, waiting for transfers between devices, shards(): summed = lax.psum_scatter(partial, 'row', scatter_dimension=0, tiled=True)  34 us
    dot_general x1, matrix products, shards(): lax.dot_general(masked_inverse, row_band, (((0,), (0,)), ((), ())), preci...  7.71 us
    concatenate x1, other arithmetic, shards(): jnp.concatenate([jnp.concatenate([tile_at(i, j) if i >= j else tile_at(j,...  5.86 us
  transfers between devices with their start and end apart: 4, of which 3 were waited for; matrix products, arithmetic and copies ran while one was open for 2% of the time, Pallas kernels for 0%

profile of v1, /device:TPU:0, one launch (start us, length us, event | category | flops | bytes accessed | tf_op | source)
XLA Modules:
  0.0 283.7 jit_solution(13454574597120912995)
XLA Ops:
  7.2 0.0 all-gather.2.cloned.1.call-start
  7.2 0.9 convert_reduce_fusion
  8.1 0.1 broadcast_bitcast_fusion
  8.2 4.3 %fusion.6 = f32[128,1024]{1,0:T(8,128)} fusion(f32[128,1024]{1,0:T(8,128)} %param.6, f32[1024]{0:T(1024)S(1)} %bitcast.21, f32[1024,1024]{1,0:T(8,128)} %param.7), kind=kOutput, calls=%fused_computation.22 | convolution fusion | flops 810680320 | bytes 5246976 | tf_op jit(solution)/shard_map/dot_general | solution.py:22
  12.5 0.0 all-gather.2.cloned.1.call-update
  12.5 0.0 reduce-scatter.2.cloned.1.call-start
  12.6 0.8 dynamic-slice_convert_fusion
  13.4 0.6 mul.36
  14.0 0.2 copy.21
  14.2 48.4 %all-gather.2.cloned.1.call-done = f32[1024,1024]{1,0:T(8,128)} async-done(((f32[128,1024]{1,0:T(8,128)}), f32[1024,1024]{1,0:T(8,128)}) %all-gather.2.cloned.1.call-update) | async-done | bytes 4194320 | tf_op jit(solution)/shard_map/all_gather | solution.py:23
  62.5 7.7 %fusion.2 = f32[512,1024]{1,0:T(8,128)} fusion(f32[1024,1024]{1,0:T(8,128)} %all-gather.2.cloned.1.call-done, f32[1024,512]{1,0:T(8,128)} %param.5, f32[1024,512]{1,0:T(8,128)S(1)} %bitcast.15), kind=kOutput, calls=%fused_computation.12 | convolution fusion | flops 3222274048 | bytes 10485760 | tf_op jit(solution)/shard_map/dot_general | solution.py:33
  70.2 0.0 reduce-scatter.2.cloned.1.call-update
  70.3 0.0 all-reduce.2.cloned.1.call-start
  70.3 0.0 copy-start
  70.3 34.0 %reduce-scatter.2.cloned.1.call-done = f32[128,1024]{1,0:T(8,128)} async-done(((f32[512,1024]{1,0:T(8,128)}), f32[128,1024]{1,0:T(8,128)}) %reduce-scatter.2.cloned.1.call-update) | async-done | bytes 524304 | tf_op jit(solution)/shard_map/reduce_scatter | solution.py:34
  104.3 1.7 collective-permute-start
  106.0 2.7 convert_add_fusion
  108.8 0.0 collective-permute-done
  108.8 0.0 copy-start.2
  108.8 0.0 copy-done
  108.8 0.4 fusion.12
  109.3 0.6 fusion.9
  109.8 0.6 fusion.5
  110.5 0.4 convolution_dynamic-update-slice_fusion
  110.9 0.0 copy-done.2
  111.2 0.0 copy-start.1
  111.2 1.5 copy-done.1
  112.7 0.0 all-reduce.2.cloned.1.call-update
  112.7 153.9 %all-reduce.2.cloned.1.call-done = f32[2560,256]{1,0:T(8,128)} async-done(((f32[2560,256]{1,0:T(8,128)}), f32[2560,256]{1,0:T(8,128)}) %all-reduce.2.cloned.1.call-update) | async-done | bytes 2621456 | tf_op jit(solution)/shard_map/psum | solution.py:48
  266.6 2.8 fusion.28
  269.4 0.1 copy.16
  269.6 0.1 copy.19
  269.7 0.1 pad_maximum_fusion.1
  269.8 0.3 copy.15
  270.1 0.1 copy.18
  270.2 0.1 copy.17
  270.4 0.1 copy.20
  270.5 0.0 copy-start.3
  270.5 5.9 %maximum_maximum_fusion = f32[1024,1024]{1,0:T(8,128)} fusion(f32[256,256]{1,0:T(8,128)} %get-tuple-element.12, f32[256,256]{1,0:T(8,128)S(1)} %get-tuple-element.13, f32[256,256]{1,0:T(8,128)} %get-tuple-element.11, f32[256,256]{1,0:T(8,128)S(1)} %get-tuple-element.6, f32[256,256]{1,0:T(8,128)S(1)} %bitcast.20, f32[256,256]{1,0:T(8,128)} %get-tuple-element.10, ...), kind=kLoop, calls=%fused_computation | loop fusion | flops 12582912 | bytes 8388608 | tf_op jit(solution)/shard_map/concatenate | solution.py:50
  276.4 0.0 copy-done.3
  276.4 0.8 copy.34
  (12 shorter events, 0.2 us)
Async XLA Ops:
  7.2 55.4 %all-gather.2.cloned.1.call-start = ((), (), s32[]{:S(2)}) async-start(), calls=%async_computation.1 | async-start | bytes 4718592 | tf_op jit(solution)/shard_map/all_gather | solution.py:23
  12.5 91.8 %reduce-scatter.2.cloned.1.call-start = ((), (), s32[]{:S(2)}) async-start(), calls=%async_computation.2 | async-start | bytes 2621440 | tf_op jit(solution)/shard_map/reduce_scatter | solution.py:34
  70.3 196.3 %all-reduce.2.cloned.1.call-start = ((), (), s32[]{:S(2)}) async-start(), calls=%async_computation.3 | async-start | bytes 5242880 | tf_op jit(solution)/shard_map/psum | solution.py:48
  70.3 38.5 %copy-start = (f32[128,1024]{1,0:T(8,128)S(1)}, f32[128,1024]{1,0:T(8,128)}, u32[]{:S(2)}) copy-start(f32[128,1024]{1,0:T(8,128)} %fusion.6) | copy-start | bytes 1572868
  104.3 4.4 %collective-permute-start = (f32[128,1024]{1,0:T(8,128)}, f32[128,1024]{1,0:T(8,128)S(1)}, u32[]{:S(2)}, u32[]{:S(2)}) collective-permute-start(f32[128,1024]{1,0:T(8,128)} %reduce-scatter.2.cloned.1.call-done), channel_id=1, source_target_pairs={{0,0},{1,4},{2,8},{3,12},{4,16},{5,20},{6,24},{7,28},{8,1},{9,5},{... | collective-permute-start | bytes 1572872 | tf_op jit(solution)/shard_map/ppermute | solution.py:36
  108.8 2.1 copy-start.2
  111.2 1.5 copy-start.1
  270.5 5.9 %copy-start.3 = (f32[128,1024]{1,0:T(8,128)S(1)}, f32[128,1024]{1,0:T(8,128)}, u32[]{:S(2)}) copy-start(f32[128,1024]{1,0:T(8,128)} %copy-done.2) | copy-start | bytes 1572868
Sparse Core Ops, SparseCore 0:
  12.7 49.8 all-gather.1
  70.4 33.9 reduce-scatter.1
  112.8 153.7 all-reduce.1

commit v2 on v1

v2 whole, which is shorter than its diff:
```python
import functools

import jax
import jax.numpy as jnp
from jax import lax
from jax.experimental import pallas as pl
from jax.experimental.pallas import tpu as pltpu
from jax.sharding import PartitionSpec as P

TILE = 256
SHARE = 32


HIGH = lax.Precision.HIGH
MESH = pl.DeviceIdType.MESH


def halves(value):
    top = value.astype(jnp.bfloat16)
    return top, (value - top.astype(jnp.float32)).astype(jnp.bfloat16)


def product(left, right, dims):
    dot = lambda a, b: lax.dot_general(a, b, (dims, ((), ())), preferred_element_type=jnp.float32)
    return dot(left[0], right[0]) + (dot(left[0], right[1]) + dot(left[1], right[0]))


def body(
    chunk_rows, flags_ref, inv_ref, x_ref, f_ref, sigma_ref, diag_ref,
    at_high, at_low, l_high, l_low, band, partial, got_part, moved, raw,
    tiles, got_core, sums, got_row, got_line, whole,
    chain_send, chain_recv, swap_send, swap_recv, part_send, part_recv, move_send, move_recv,
    sum_send, core_recv, row_recv, line_recv, back_line, back_row, back_core,
):
    rows_n, cols_n = lax.axis_size("row"), lax.axis_size("col")
    line_n = cols_n // 2
    row, col = lax.axis_index("row"), lax.axis_index("col")
    line, core = col // 2, col % 2
    block_rows, block_cols = inv_ref.shape
    piece_rows, width = x_ref.shape
    count = width // TILE
    other_core = (row, 2 * line + 1 - core)
    row_peers = [((row + d) % rows_n, col) for d in range(1, rows_n)]
    line_peers = [(row, 2 * ((line + d) % line_n) + core) for d in range(1, line_n)]
    peers = [other_core] + row_peers + line_peers
    target_at = col * rows_n + row
    target = (target_at // cols_n, target_at % cols_n)
    own_at = row * cols_n + col
    source = (own_at % rows_n, own_at // rows_n)
    stays = target_at == own_at

    barrier = pltpu.get_barrier_semaphore()
    for peer in peers:
        pl.semaphore_signal(barrier, inc=1, device_id=peer, device_id_type=MESH)

    @pl.when(jnp.logical_not(stays))
    def _():
        pl.semaphore_signal(barrier, inc=1, device_id=source, device_id_type=MESH)

    for j in range(count):
        band[j, pl.ds(pl.multiple_of(col * piece_rows, 8), piece_rows)] = x_ref[:, j * TILE : (j + 1) * TILE]

    @pl.when(stays)
    def _():
        pl.semaphore_wait(barrier, len(peers))

    @pl.when(jnp.logical_not(stays))
    def _():
        pl.semaphore_wait(barrier, len(peers) + 1)

    def span(start, size):
        return pl.ds(pl.multiple_of(start, 8), size)

    def remote(src, dst, send_sem, recv_sem, peer):
        return pltpu.make_async_remote_copy(
            src_ref=src, dst_ref=dst, send_sem=send_sem, recv_sem=recv_sem, device_id=peer, device_id_type=MESH
        )

    def begin(src, dst, send_sem, recv_sem, peer):
        copy = remote(src, dst, send_sem, recv_sem, peer)
        copy.start()
        return copy

    def prepare():
        for a in range(block_rows // TILE):
            for b in range(block_cols // TILE):
                flag = flags_ref[row * (block_rows // TILE) + a, col * (block_cols // TILE) + b].astype(jnp.float32)
                tile = inv_ref[a * TILE : (a + 1) * TILE, b * TILE : (b + 1) * TILE] * flag
                top, rest = halves(tile.T)
                at_high[b * TILE : (b + 1) * TILE, a * TILE : (a + 1) * TILE] = top
                at_low[b * TILE : (b + 1) * TILE, a * TILE : (a + 1) * TILE] = rest
        top, rest = halves(jnp.concatenate([x_ref[...], f_ref[...]], axis=0))
        l_high[...] = top
        l_low[...] = rest

    def chunk(j):
        def piece_of(at, k):
            return band.at[j, span((2 * at + k) * piece_rows, piece_rows)]

        def hop(way, s):
            begun = line - way * (s - 1)
            came = line - way * s
            n = 0 if way > 0 else 1
            go = (line + way >= 0) & (line + way < line_n) & (begun >= 0) & (begun < line_n)
            arrives = (came >= 0) & (came < line_n)
            sem = (j, n, s)
            return go, arrives, begun, came, sem

        def hop_copy(at, sem, way):
            place = piece_of(at, core)
            return remote(place, place, chain_send.at[sem], chain_recv.at[sem], (row, 2 * (line + way) + core))

        def swap(at, slot):
            place = piece_of(at, core)
            return remote(place, place, swap_send.at[j, slot], swap_recv.at[j, slot], other_core)

        for s in range(1, line_n):
            for way in (1, -1):
                go, _, begun, _, sem = hop(way, s)

                @pl.when(go)
                def _():
                    hop_copy(begun, sem, way).start()

            if s == 1:
                swap(line, 0).start()
            yield
            for way in (1, -1):
                _, arrives, _, came, sem = hop(way, s)
                slot = 2 * s - 1 if way > 0 else 2 * s

                @pl.when(arrives)
                def _():
                    hop_copy(came, sem, way).wait_recv()
                    swap(came, slot).start()

        for s in range(1, line_n):
            for way in (1, -1):
                go, arrives, begun, came, sem = hop(way, s)
                slot = 2 * s - 1 if way > 0 else 2 * s

                @pl.when(go)
                def _():
                    hop_copy(begun, sem, way).wait_send()

                @pl.when(arrives)
                def _():
                    swap(came, slot).wait()

        swap(line, 0).wait()
        partial[j] = product((at_high[...], at_low[...]), halves(band[j]), ((1,), (0,)))
        copies = []
        for d in range(1, rows_n):
            to = (row + d) % rows_n
            src = partial.at[j, span(to * piece_rows, piece_rows)]
            copies.append(begin(src, got_part.at[j, d], part_send.at[j, d], part_recv.at[j, d], row_peers[d - 1]))
        yield
        for copy in copies:
            copy.wait()
        value = partial[j, span(row * piece_rows, piece_rows)]
        for d in range(1, rows_n):
            value = value + got_part[j, d]
        raw[j] = value
        move = lambda: remote(raw.at[j], moved.at[j], move_send.at[j], move_recv.at[j], target)

        @pl.when(jnp.logical_not(stays))
        def _():
            move().start()

        @pl.when(stays)
        def _():
            moved[j] = raw[j]

        yield

        @pl.when(jnp.logical_not(stays))
        def _():
            move().wait()

        here = slice(j * TILE, (j + 1) * TILE)
        sigma_ref[:, here] = -moved[j]
        full = (count - j) * TILE
        total = chunk_rows[j]
        base = sum(chunk_rows[:j])
        right = halves(jnp.concatenate([moved[j], f_ref[:, here]], axis=0))
        tiles[base : base + full] = product((l_high[:, j * TILE :], l_low[:, j * TILE :]), right, ((0,), (0,)))
        if total > full:
            tiles[base + full : base + total] = jnp.zeros((total - full, TILE), jnp.float32)
        half, part = total // 2, total // (2 * rows_n)
        piece = part // line_n
        base_half, base_part, base_piece = base // 2, base // (2 * rows_n), base // (2 * rows_n * line_n)
        src = tiles.at[span(base + (1 - core) * half, half)]
        copy = begin(src, got_core.at[base_half : base_half + half], sum_send.at[j, 0], core_recv.at[j], other_core)
        yield
        copy.wait()
        own = span(base + core * half, half)
        sums[base_half : base_half + half] = tiles[own] + got_core[base_half : base_half + half]
        here_part = slice(base_part, base_part + part)
        copies = []
        for d in range(1, rows_n):
            to = (row + d) % rows_n
            src = sums.at[span(base_half + to * part, part)]
            copies.append(
                begin(src, got_row.at[d, here_part], sum_send.at[j, d], row_recv.at[j, d], row_peers[d - 1])
            )
        yield
        for copy in copies:
            copy.wait()
        value = sums[span(base_half + row * part, part)]
        for d in range(1, rows_n):
            value = value + got_row[d, here_part]
        got_row[0, here_part] = value
        here_piece = slice(base_piece, base_piece + piece)
        copies = []
        for d in range(1, line_n):
            to = (line + d) % line_n
            src = got_row.at[0, span(base_part + to * piece, piece)]
            copies.append(
                begin(src, got_line.at[d, here_piece], sum_send.at[j, d], line_recv.at[j, d], line_peers[d - 1])
            )
        yield
        for copy in copies:
            copy.wait()
        value = got_row[0, span(base_part + line * piece, piece)]
        for d in range(1, line_n):
            value = value + got_line[d, here_piece]
        mine = span(base + core * half + row * part + line * piece, piece)
        whole[mine] = value
        copies = [
            begin(whole.at[mine], whole.at[mine], sum_send.at[j, d], back_line.at[j, d], line_peers[d - 1])
            for d in range(1, line_n)
        ]
        yield
        for copy in copies:
            copy.wait()
        mine = span(base + core * half + row * part, part)
        copies = [
            begin(whole.at[mine], whole.at[mine], sum_send.at[j, d], back_row.at[j, d], row_peers[d - 1])
            for d in range(1, rows_n)
        ]
        yield
        for copy in copies:
            copy.wait()
        mine = span(base + core * half, half)
        copy = begin(whole.at[mine], whole.at[mine], sum_send.at[j, 0], back_core.at[j], other_core)
        yield
        copy.wait()
        for i in range(j, count):
            tile = whole[base + (i - j) * TILE : base + (i - j + 1) * TILE]
            diag_ref[i * TILE : (i + 1) * TILE, here] = tile
            if i != j:
                diag_ref[here, i * TILE : (i + 1) * TILE] = tile.T

    waiting = [chunk(j) for j in range(count)]
    active = []
    first = True
    while waiting or active:
        if waiting:
            active.append(waiting.pop(0))
        active = [flow for flow in active if next(flow, "end") != "end"]
        if first:
            prepare()
            first = False


def finish(pattern, inverse, scaled, factor_rows):
    rows_n = lax.axis_size("row")
    cols_n = lax.axis_size("col")
    line_n = cols_n // 2
    piece_rows, width = scaled.shape
    block_rows, block_cols = inverse.shape
    count = width // TILE
    shares = 2 * rows_n * line_n
    chunk_rows = tuple(-(-(count - j) * TILE // (8 * shares)) * 8 * shares for j in range(count))
    total = sum(chunk_rows)
    most = max(rows_n, line_n)
    dma = pltpu.SemaphoreType.DMA
    vmem = pl.BlockSpec(memory_space=pltpu.VMEM)
    f32, b16 = jnp.float32, jnp.bfloat16
    return pl.pallas_call(
        functools.partial(body, chunk_rows),
        out_shape=(
            jax.ShapeDtypeStruct((piece_rows, width), f32),
            jax.ShapeDtypeStruct((width, width), f32),
        ),
        in_specs=[pl.BlockSpec(memory_space=pltpu.SMEM), vmem, vmem, vmem],
        out_specs=(vmem, vmem),
        scratch_shapes=[
            pltpu.VMEM((block_cols, block_rows), b16),
            pltpu.VMEM((block_cols, block_rows), b16),
            pltpu.VMEM((piece_rows + SHARE, width), b16),
            pltpu.VMEM((piece_rows + SHARE, width), b16),
            pltpu.VMEM((count, block_rows, TILE), f32),
            pltpu.VMEM((count, block_cols, TILE), f32),
            pltpu.VMEM((count, rows_n, piece_rows, TILE), f32),
            pltpu.VMEM((count, piece_rows, TILE), f32),
            pltpu.VMEM((count, piece_rows, TILE), f32),
            pltpu.VMEM((total, TILE), f32),
            pltpu.VMEM((total // 2, TILE), f32),
            pltpu.VMEM((total // 2, TILE), f32),
            pltpu.VMEM((rows_n, total // (2 * rows_n), TILE), f32),
            pltpu.VMEM((line_n, total // shares, TILE), f32),
            pltpu.VMEM((total, TILE), f32),
            dma((count, 2, line_n)),
            dma((count, 2, line_n)),
            dma((count, 2 * line_n)),
            dma((count, 2 * line_n)),
            dma((count, rows_n)),
            dma((count, rows_n)),
            dma((count,)),
            dma((count,)),
            dma((count, most)),
            dma((count,)),
            dma((count, rows_n)),
            dma((count, line_n)),
            dma((count, line_n)),
            dma((count, rows_n)),
            dma((count,)),
        ],
        compiler_params=pltpu.CompilerParams(collective_id=0, has_side_effects=True, vmem_limit_bytes=56 << 20),
    )(pattern, inverse, scaled, factor_rows)


def shards(ancestor_inverse, panel, diag_inverse, inverse_pattern, panel_pattern):
    rows_count = lax.axis_size("row")
    cols_count = lax.axis_size("col")
    piece_rows, panel_width = panel.shape
    place = lax.axis_index("row") * cols_count + lax.axis_index("col")
    inv_factor = jnp.tril(diag_inverse) + jnp.eye(panel_width, dtype=jnp.float32)
    row_flags = lax.dynamic_slice_in_dim(panel_pattern, place * piece_rows // TILE, 1, 0).astype(jnp.float32)
    local_scaled = jnp.dot(panel * jnp.repeat(row_flags, TILE, axis=1), inv_factor, precision=HIGH)
    share = panel_width // (rows_count * cols_count)
    factor_rows = lax.dynamic_slice_in_dim(inv_factor, place * share, share, 0)
    if share < SHARE:
        factor_rows = jnp.pad(factor_rows, ((0, SHARE - share), (0, 0)))
    return finish(inverse_pattern, ancestor_inverse, local_scaled, factor_rows)


def solution(mesh):
    return jax.shard_map(
        shards,
        mesh=mesh,
        in_specs=(P("row", "col"), P(("row", "col"), None), P(), P(), P()),
        out_specs=(P(("row", "col"), None), P()),
        check_vma=False,
    )
```

time: 284 us -> 126 us (0.44)
  waiting for transfers between devices: 236 us -> 0 us
  Pallas kernels: 0 us -> 111 us
  between operations: 14 us -> 0.68 us
  matrix products: 14.1 us -> 4.48 us
  other arithmetic: 10.3 us -> 1.7 us
    psum x1 -> x0, waiting for transfers between devices: 154 us -> none  [shards(): summed_tiles = lax.psum(jnp.concatenate(bands, axis=0), ('row', 'col'))]
    pallas_call x0 -> x1, Pallas kernels: none -> 111 us  [finish(): pl.pallas_call(functools.partial(body, chunk_rows), out_shape=(jax.ShapeD...]
    all_gather x1 -> x0, waiting for transfers between devices: 48.4 us -> none  [shards(): row_band = lax.all_gather(local_scaled, 'col', axis=0, tiled=True)]
    reduce_scatter x1 -> x0, waiting for transfers between devices: 34 us -> none  [shards(): summed = lax.psum_scatter(partial, 'row', scatter_dimension=0, tiled=True)]
    dot_general x5 -> x0, matrix products: 9.76 us -> none  [the longest x1 7.71 us: shards(): lax.dot_general(masked_inverse, row_band, (((0,), (0,)), ((), ())), preci...]
    concatenate x2 -> x0, other arithmetic: 5.93 us -> none  [the longest x1 5.86 us: shards(): jnp.concatenate([jnp.concatenate([tile_at(i, j) if i >= j else tile_at(j,...]
    unnamed x25 -> x6, local copies, waits for them, and re-layouts: 3.34 us -> 6.76 us
  transfers between devices with their start and end apart: 4 -> 0, of which waited for: 3 -> 0; matrix products, arithmetic and copies ran while one was open for 2% -> 0% of each run, Pallas kernels for 0% -> 0%
where the time goes in v2:
time: 126 us; the launch traced here: 125 us
  Pallas kernels  111 us (88%)
  local copies, waits for them, and re-layouts  7.43 us (6%)
  matrix products  4.48 us (4%)
  other arithmetic  1.7 us (1%)
    pallas_call x1, Pallas kernels, finish(): pl.pallas_call(functools.partial(body, chunk_rows), out_shape=(jax.ShapeD...  111 us
    unnamed x6, local copies, waits for them, and re-layouts  6.76 us
    dot_general x1, matrix products, shards(): jnp.dot(panel * jnp.repeat(row_flags, TILE, axis=1), inv_factor, precisio...  4.48 us

profile of v2, /device:TPU:0, one launch (start us, length us, event | category | flops | bytes accessed | tf_op | source)
XLA Modules:
  0.0 125.4 jit_solution(8629771410206739369)
XLA Ops:
  0.7 0.0 copy-start
  0.7 1.0 convert_reduce_fusion
  1.7 0.1 broadcast_bitcast_fusion
  1.8 4.5 %fusion.x_ref = f32[128,1024]{1,0:T(8,128)} fusion(f32[128,1024]{1,0:T(8,128)} %param.6, f32[1024]{0:T(1024)S(1)} %bitcast.3, f32[1024,1024]{1,0:T(8,128)} %param.7), kind=kOutput, calls=%fused_computation.3 | convolution fusion | flops 810680320 | bytes 5246976 | tf_op jit(solution)/shard_map/dot_general | solution.py:331
  6.2 0.0 copy-done
  6.2 0.7 convert_add_fusion
  6.9 0.7 constant_dynamic-slice_fusion.f_ref
  7.6 111.1 %shard_map.68 = (f32[128,1024]{1,0:T(8,128)}, f32[1024,1024]{1,0:T(8,128)}) custom-call(s32[16,16]{1,0:T(8,128)} %flags_ref.1, f32[1024,512]{1,0:T(8,128)} %inv_ref.1, f32[128,1024]{1,0:T(8,128)} %fusion.x_ref, f32[32,1024]{1,0:T(8,128)} %constant_dynamic-slice_fusion.f_ref), custom_call_target="tpu_custom_call" | custom-call | tf_op jit(solution)/shard_map/pallas_call | solution.py:280
  118.7 1.9 %copy.10 = f32[128,1024]{1,0:T(8,128)} copy(f32[128,1024]{1,0:T(8,128)} %get-tuple-element.4) | data formatting | bytes 1048576
  120.6 4.8 %copy.11 = f32[1024,1024]{1,0:T(8,128)} copy(f32[1024,1024]{1,0:T(8,128)} %get-tuple-element.5) | data formatting | bytes 8388608
  (1 shorter events, 0.0 us)
Async XLA Ops:
  0.7 5.6 %copy-start = (f32[1024,1024]{1,0:T(8,128)S(1)}, f32[1024,1024]{1,0:T(8,128)}, u32[]{:S(2)}) copy-start(f32[1024,1024]{1,0:T(8,128)} %param.7) | copy-start | bytes 12582916

commit v3 on v2

--- a/solution.py
+++ b/solution.py
@@ -11,7 +11,6 @@
 SHARE = 32
 
 
-HIGH = lax.Precision.HIGH
 MESH = pl.DeviceIdType.MESH
 
 
@@ -26,9 +25,9 @@
 
 
 def body(
-    chunk_rows, flags_ref, inv_ref, x_ref, f_ref, sigma_ref, diag_ref,
-    at_high, at_low, l_high, l_low, band, partial, got_part, moved, raw,
-    tiles, got_core, sums, got_row, got_line, whole,
+    chunk_rows, flags_ref, panel_flags_ref, inv_ref, panel_ref, factor_ref, moved, whole,
+    at_high, at_low, p_high, p_low, l_high, l_low, f_ref, band, partial, got_part, raw,
+    tiles, got_core, sums, got_row, got_line,
     chain_send, chain_recv, swap_send, swap_recv, part_send, part_recv, move_send, move_recv,
     sum_send, core_recv, row_recv, line_recv, back_line, back_row, back_core,
 ):
@@ -37,7 +36,7 @@
     row, col = lax.axis_index("row"), lax.axis_index("col")
     line, core = col // 2, col % 2
     block_rows, block_cols = inv_ref.shape
-    piece_rows, width = x_ref.shape
+    piece_rows, width = panel_ref.shape
     count = width // TILE
     other_core = (row, 2 * line + 1 - core)
     row_peers = [((row + d) % rows_n, col) for d in range(1, rows_n)]
@@ -57,8 +56,18 @@
     def _():
         pl.semaphore_signal(barrier, inc=1, device_id=source, device_id_type=MESH)
 
-    for j in range(count):
-        band[j, pl.ds(pl.multiple_of(col * piece_rows, 8), piece_rows)] = x_ref[:, j * TILE : (j + 1) * TILE]
+    share = width // (rows_n * cols_n)
+    first = own_at * share
+    start = first // SHARE * SHARE
+    ids = start + lax.broadcasted_iota(jnp.int32, (SHARE, width), 0)
+    places = lax.broadcasted_iota(jnp.int32, (SHARE, width), 1)
+    rows = jnp.where(ids >= places, factor_ref[pl.ds(pl.multiple_of(start, 8), SHARE)], 0.0)
+    rows = rows + jnp.where(ids == places, 1.0, 0.0)
+    f_ref[...] = jnp.where((ids >= first) & (ids < first + share), rows, 0.0)
+    for k in range(count):
+        here = slice(k * TILE, (k + 1) * TILE)
+        flag = panel_flags_ref[own_at * piece_rows // TILE, k].astype(jnp.float32)
+        p_high[:, here], p_low[:, here] = halves(panel_ref[:, here] * flag)
 
     @pl.when(stays)
     def _():
@@ -89,11 +98,19 @@
                 top, rest = halves(tile.T)
                 at_high[b * TILE : (b + 1) * TILE, a * TILE : (a + 1) * TILE] = top
                 at_low[b * TILE : (b + 1) * TILE, a * TILE : (a + 1) * TILE] = rest
-        top, rest = halves(jnp.concatenate([x_ref[...], f_ref[...]], axis=0))
-        l_high[...] = top
-        l_low[...] = rest
 
     def chunk(j):
+        here = slice(j * TILE, (j + 1) * TILE)
+        ids = lax.broadcasted_iota(jnp.int32, (TILE, TILE), 0)
+        places = lax.broadcasted_iota(jnp.int32, (TILE, TILE), 1)
+        corner = jnp.where(ids >= places, factor_ref[here, here], 0.0) + jnp.where(ids == places, 1.0, 0.0)
+        factor = corner
+        if j + 1 < count:
+            factor = jnp.concatenate([corner, factor_ref[(j + 1) * TILE :, here]], axis=0)
+        scaled = product((p_high[:, j * TILE :], p_low[:, j * TILE :]), halves(factor), ((1,), (0,)))
+        band[j, span(col * piece_rows, piece_rows)] = scaled
+        l_high[:, here], l_low[:, here] = halves(jnp.concatenate([scaled, f_ref[:, here]], axis=0))
+
         def piece_of(at, k):
             return band.at[j, span((2 * at + k) * piece_rows, piece_rows)]
 
@@ -177,8 +194,6 @@
         def _():
             move().wait()
 
-        here = slice(j * TILE, (j + 1) * TILE)
-        sigma_ref[:, here] = -moved[j]
         full = (count - j) * TILE
         total = chunk_rows[j]
         base = sum(chunk_rows[:j])
@@ -245,11 +260,6 @@
         copy = begin(whole.at[mine], whole.at[mine], sum_send.at[j, 0], back_core.at[j], other_core)
         yield
         copy.wait()
-        for i in range(j, count):
-            tile = whole[base + (i - j) * TILE : base + (i - j + 1) * TILE]
-            diag_ref[i * TILE : (i + 1) * TILE, here] = tile
-            if i != j:
-                diag_ref[here, i * TILE : (i + 1) * TILE] = tile.T
 
     waiting = [chunk(j) for j in range(count)]
     active = []
@@ -263,11 +273,27 @@
             first = False
 
 
-def finish(pattern, inverse, scaled, factor_rows):
+def write_out(chunk_rows, moved, whole, sigma_ref, diag_ref):
+    count = moved.shape[0]
+    step_rows = sigma_ref.shape[0]
+    step = pl.program_id(0)
+    for i in range(count):
+
+        @pl.when(step == i)
+        def _():
+            for j in range(count):
+                low, high = min(i, j), max(i, j)
+                at = sum(chunk_rows[:low]) + (high - low) * TILE
+                tile = whole[at : at + TILE]
+                diag_ref[:, j * TILE : (j + 1) * TILE] = tile if i >= j else tile.T
+                sigma_ref[:, j * TILE : (j + 1) * TILE] = -moved[j, i * step_rows : (i + 1) * step_rows]
+
+
+def finish(pattern, panel_pattern, inverse, panel, factor):
     rows_n = lax.axis_size("row")
     cols_n = lax.axis_size("col")
     line_n = cols_n // 2
-    piece_rows, width = scaled.shape
+    piece_rows, width = panel.shape
     block_rows, block_cols = inverse.shape
     count = width // TILE
     shares = 2 * rows_n * line_n
@@ -276,31 +302,33 @@
     most = max(rows_n, line_n)
     dma = pltpu.SemaphoreType.DMA
     vmem = pl.BlockSpec(memory_space=pltpu.VMEM)
+    smem = pl.BlockSpec(memory_space=pltpu.SMEM)
     f32, b16 = jnp.float32, jnp.bfloat16
-    return pl.pallas_call(
+    moved, whole = pl.pallas_call(
         functools.partial(body, chunk_rows),
         out_shape=(
-            jax.ShapeDtypeStruct((piece_rows, width), f32),
-            jax.ShapeDtypeStruct((width, width), f32),
+            jax.ShapeDtypeStruct((count, piece_rows, TILE), f32),
+            jax.ShapeDtypeStruct((total, TILE), f32),
         ),
-        in_specs=[pl.BlockSpec(memory_space=pltpu.SMEM), vmem, vmem, vmem],
+        in_specs=[smem, smem, vmem, vmem, vmem],
         out_specs=(vmem, vmem),
         scratch_shapes=[
             pltpu.VMEM((block_cols, block_rows), b16),
             pltpu.VMEM((block_cols, block_rows), b16),
+            pltpu.VMEM((piece_rows, width), b16),
+            pltpu.VMEM((piece_rows, width), b16),
             pltpu.VMEM((piece_rows + SHARE, width), b16),
             pltpu.VMEM((piece_rows + SHARE, width), b16),
+            pltpu.VMEM((SHARE, width), f32),
             pltpu.VMEM((count, block_rows, TILE), f32),
             pltpu.VMEM((count, block_cols, TILE), f32),
             pltpu.VMEM((count, rows_n, piece_rows, TILE), f32),
-            pltpu.VMEM((count, piece_rows, TILE), f32),
             pltpu.VMEM((count, piece_rows, TILE), f32),
             pltpu.VMEM((total, TILE), f32),
             pltpu.VMEM((total // 2, TILE), f32),
             pltpu.VMEM((total // 2, TILE), f32),
             pltpu.VMEM((rows_n, total // (2 * rows_n), TILE), f32),
             pltpu.VMEM((line_n, total // shares, TILE), f32),
-            pltpu.VMEM((total, TILE), f32),
             dma((count, 2, line_n)),
             dma((count, 2, line_n)),
             dma((count, 2 * line_n)),
@@ -318,22 +346,25 @@
             dma((count,)),
         ],
         compiler_params=pltpu.CompilerParams(collective_id=0, has_side_effects=True, vmem_limit_bytes=56 << 20),
-    )(pattern, inverse, scaled, factor_rows)
+    )(pattern, panel_pattern, inverse, panel, factor)
+    return pl.pallas_call(
+        functools.partial(write_out, chunk_rows),
+        grid=(count,),
+        out_shape=(jax.ShapeDtypeStruct((piece_rows, width), f32), jax.ShapeDtypeStruct((width, width), f32)),
+        in_specs=[
+            pl.BlockSpec((count, piece_rows, TILE), lambda i: (0, 0, 0)),
+            pl.BlockSpec((total, TILE), lambda i: (0, 0)),
+        ],
+        out_specs=(
+            pl.BlockSpec((piece_rows // count, width), lambda i: (i, 0)),
+            pl.BlockSpec((TILE, width), lambda i: (i, 0)),
+        ),
+        compiler_params=pltpu.CompilerParams(vmem_limit_bytes=32 << 20),
+    )(moved, whole)
 
 
 def shards(ancestor_inverse, panel, diag_inverse, inverse_pattern, panel_pattern):
-    rows_count = lax.axis_size("row")
-    cols_count = lax.axis_size("col")
-    piece_rows, panel_width = panel.shape
-    place = lax.axis_index("row") * cols_count + lax.axis_index("col")
-    inv_factor = jnp.tril(diag_inverse) + jnp.eye(panel_width, dtype=jnp.float32)
-    row_flags = lax.dynamic_slice_in_dim(panel_pattern, place * piece_rows // TILE, 1, 0).astype(jnp.float32)
-    local_scaled = jnp.dot(panel * jnp.repeat(row_flags, TILE, axis=1), inv_factor, precision=HIGH)
-    share = panel_width // (rows_count * cols_count)
-    factor_rows = lax.dynamic_slice_in_dim(inv_factor, place * share, share, 0)
-    if share < SHARE:
-        factor_rows = jnp.pad(factor_rows, ((0, SHARE - share), (0, 0)))
-    return finish(inverse_pattern, ancestor_inverse, local_scaled, factor_rows)
+    return finish(inverse_pattern, panel_pattern, ancestor_inverse, panel, diag_inverse)
 
 
 def solution(mesh):

time: 126 us -> 121 us (0.960)
  Pallas kernels: 111 us -> 116 us
  matrix products: 4.48 us -> 0 us
  local copies, waits for them, and re-layouts: 7.43 us -> 4.13 us
  other arithmetic: 1.7 us -> 0 us
    dot_general x1 -> x0, matrix products: 4.48 us -> none  [shards(): jnp.dot(panel * jnp.repeat(row_flags, TILE, axis=1), inv_factor, precisio...]
    pallas_call x0 -> x1, Pallas kernels: none -> 2.83 us  [finish(): pl.pallas_call(functools.partial(write_out, chunk_rows), grid=(count,), o...]
    unnamed x6 -> x5, local copies, waits for them, and re-layouts: 6.76 us -> 4.13 us
    pallas_call x1, Pallas kernels: 111 us -> 113 us  [finish(): pl.pallas_call(functools.partial(body, chunk_rows), out_shape=(jax.ShapeD...]
where the time goes in v3:
time: 121 us; the launch traced here: 120 us
  Pallas kernels  116 us (96%)
  local copies, waits for them, and re-layouts  4.13 us (3%)
    pallas_call x1, Pallas kernels, finish(): pl.pallas_call(functools.partial(body, chunk_rows), out_shape=(jax.ShapeD...  113 us
    unnamed x5, local copies, waits for them, and re-layouts  4.13 us
    pallas_call x1, Pallas kernels, finish(): pl.pallas_call(functools.partial(write_out, chunk_rows), grid=(count,), o...  2.83 us

profile of v3, /device:TPU:0, one launch (start us, length us, event | category | flops | bytes accessed | tf_op | source)
XLA Modules:
  0.0 120.4 jit_solution(11711396462341135865)
XLA Ops:
  0.6 1.4 %copy.7.panel_flags_ref = s32[16,4]{1,0:T(8,128)} copy(s32[16,4]{0,1:T(4,128)} %param.9) | data formatting | bytes 512 | tf_op args[4]
  2.0 112.7 %shard_map.68 = (f32[4,128,256]{2,1,0:T(8,128)}, f32[2560,256]{1,0:T(8,128)}) custom-call(s32[16,16]{1,0:T(8,128)} %flags_ref.1, s32[16,4]{1,0:T(8,128)} %copy.7.panel_flags_ref, f32[1024,512]{1,0:T(8,128)} %inv_ref.1, f32[128,1024]{1,0:T(8,128)} %panel_ref.1, f32[1024,1024]{1,0:T(8,128)} %factor_ref.1), custom_call_target="tpu_custom_call" | custom-call | tf_op jit(solution)/shard_map/pallas_call | solution.py:307
  114.7 0.0 copy-start
  114.7 1.7 %copy-done = f32[2560,256]{1,0:T(8,128)S(1)} copy-done((f32[2560,256]{1,0:T(8,128)S(1)}, f32[2560,256]{1,0:T(8,128)}, u32[]{:S(2)}) %copy-start) | copy-done | bytes 2621464
  116.5 0.0 copy-start.1
  116.5 1.0 copy-done.1
  117.5 2.8 %shard_map.69 = (f32[128,1024]{1,0:T(8,128)}, f32[1024,1024]{1,0:T(8,128)}) custom-call(f32[4,128,256]{2,1,0:T(8,128)S(1)} %copy-done.1, f32[2560,256]{1,0:T(8,128)S(1)} %copy-done), custom_call_target="tpu_custom_call" | custom-call | tf_op jit(solution)/shard_map/pallas_call | solution.py:350
Async XLA Ops:
  114.7 1.7 %copy-start = (f32[2560,256]{1,0:T(8,128)S(1)}, f32[2560,256]{1,0:T(8,128)}, u32[]{:S(2)}) copy-start(f32[2560,256]{1,0:T(8,128)} %get-tuple-element.5.whole) | copy-start | bytes 7864324
  116.5 1.0 copy-start.1

commit v4 on v3

--- a/solution.py
+++ b/solution.py
@@ -141,7 +141,7 @@
 
             if s == 1:
                 swap(line, 0).start()
-            yield
+            yield "line", 2 * piece_rows, 0.5
             for way in (1, -1):
                 _, arrives, _, came, sem = hop(way, s)
                 slot = 2 * s - 1 if way > 0 else 2 * s
@@ -171,7 +171,7 @@
             to = (row + d) % rows_n
             src = partial.at[j, span(to * piece_rows, piece_rows)]
             copies.append(begin(src, got_part.at[j, d], part_send.at[j, d], part_recv.at[j, d], row_peers[d - 1]))
-        yield
+        yield "plane", 4 * piece_rows * (rows_n - 1) / 3, 3.0
         for copy in copies:
             copy.wait()
         value = partial[j, span(row * piece_rows, piece_rows)]
@@ -188,7 +188,7 @@
         def _():
             moved[j] = raw[j]
 
-        yield
+        yield "plane", 2 * piece_rows, 0.5
 
         @pl.when(jnp.logical_not(stays))
         def _():
@@ -206,7 +206,7 @@
         base_half, base_part, base_piece = base // 2, base // (2 * rows_n), base // (2 * rows_n * line_n)
         src = tiles.at[span(base + (1 - core) * half, half)]
         copy = begin(src, got_core.at[base_half : base_half + half], sum_send.at[j, 0], core_recv.at[j], other_core)
-        yield
+        yield "core", half, 1.0
         copy.wait()
         own = span(base + core * half, half)
         sums[base_half : base_half + half] = tiles[own] + got_core[base_half : base_half + half]
@@ -218,7 +218,7 @@
             copies.append(
                 begin(src, got_row.at[d, here_part], sum_send.at[j, d], row_recv.at[j, d], row_peers[d - 1])
             )
-        yield
+        yield "plane", 4 * part, 0.5
         for copy in copies:
             copy.wait()
         value = sums[span(base_half + row * part, part)]
@@ -233,7 +233,7 @@
             copies.append(
                 begin(src, got_line.at[d, here_piece], sum_send.at[j, d], line_recv.at[j, d], line_peers[d - 1])
             )
-        yield
+        yield "line", 8 * piece, 0.5
         for copy in copies:
             copy.wait()
         value = got_row[0, span(base_part + line * piece, piece)]
@@ -245,7 +245,7 @@
             begin(whole.at[mine], whole.at[mine], sum_send.at[j, d], back_line.at[j, d], line_peers[d - 1])
             for d in range(1, line_n)
         ]
-        yield
+        yield "line", 8 * piece, 0.5
         for copy in copies:
             copy.wait()
         mine = span(base + core * half + row * part, part)
@@ -253,23 +253,32 @@
             begin(whole.at[mine], whole.at[mine], sum_send.at[j, d], back_row.at[j, d], row_peers[d - 1])
             for d in range(1, rows_n)
         ]
-        yield
+        yield "plane", 4 * part, 0.5
         for copy in copies:
             copy.wait()
         mine = span(base + core * half, half)
         copy = begin(whole.at[mine], whole.at[mine], sum_send.at[j, 0], back_core.at[j], other_core)
-        yield
+        yield "core", half, 0.5
         copy.wait()
 
-    waiting = [chunk(j) for j in range(count)]
-    active = []
+    free = {"line": 0.0, "plane": 0.0, "core": 0.0}
+    now = 0.0
+    events = [(4.0 * j, j, chunk(j)) for j in range(count)]
     first = True
-    while waiting or active:
-        if waiting:
-            active.append(waiting.pop(0))
-        active = [flow for flow in active if next(flow, "end") != "end"]
+    while events:
+        events.sort(key=lambda event: event[:2])
+        due, j, flow = events.pop(0)
+        now = max(now, due)
+        step = next(flow, None)
+        if step is not None:
+            link, kilobytes, work = step
+            now += work
+            rate = 300.0 if link == "core" else 85.0
+            free[link] = max(free[link], now) + kilobytes / rate
+            events.append((free[link] + 1.5, j, flow))
         if first:
             prepare()
+            now += 3.0
             first = False
 
 

time: 121 us -> 115 us (0.950)
  Pallas kernels: 116 us -> 110 us
    pallas_call x1, Pallas kernels: 113 us -> 107 us  [finish(): pl.pallas_call(functools.partial(body, chunk_rows), out_shape=(jax.ShapeD...]
where the time goes in v4:
time: 115 us; the launch traced here: 114 us
  Pallas kernels  110 us (96%)
  local copies, waits for them, and re-layouts  4.13 us (4%)
    pallas_call x1, Pallas kernels, finish(): pl.pallas_call(functools.partial(body, chunk_rows), out_shape=(jax.ShapeD...  107 us
    unnamed x5, local copies, waits for them, and re-layouts  4.13 us
    pallas_call x1, Pallas kernels, finish(): pl.pallas_call(functools.partial(write_out, chunk_rows), grid=(count,), o...  2.83 us

profile of v4, /device:TPU:0, one launch (start us, length us, event | category | flops | bytes accessed | tf_op | source)
XLA Modules:
  0.0 114.5 jit_solution(8255270454156869930)
XLA Ops:
  0.6 1.4 %copy.7.panel_flags_ref = s32[16,4]{1,0:T(8,128)} copy(s32[16,4]{0,1:T(4,128)} %param.9) | data formatting | bytes 512 | tf_op args[4]
  2.0 106.9 %shard_map.68 = (f32[4,128,256]{2,1,0:T(8,128)}, f32[2560,256]{1,0:T(8,128)}) custom-call(s32[16,16]{1,0:T(8,128)} %flags_ref.1, s32[16,4]{1,0:T(8,128)} %copy.7.panel_flags_ref, f32[1024,512]{1,0:T(8,128)} %inv_ref.1, f32[128,1024]{1,0:T(8,128)} %panel_ref.1, f32[1024,1024]{1,0:T(8,128)} %factor_ref.1), custom_call_target="tpu_custom_call" | custom-call | tf_op jit(solution)/shard_map/pallas_call | solution.py:316
  108.9 0.0 copy-start
  108.9 1.7 %copy-done = f32[2560,256]{1,0:T(8,128)S(1)} copy-done((f32[2560,256]{1,0:T(8,128)S(1)}, f32[2560,256]{1,0:T(8,128)}, u32[]{:S(2)}) %copy-start) | copy-done | bytes 2621464
  110.6 0.0 copy-start.1
  110.6 1.0 copy-done.1
  111.7 2.8 %shard_map.69 = (f32[128,1024]{1,0:T(8,128)}, f32[1024,1024]{1,0:T(8,128)}) custom-call(f32[4,128,256]{2,1,0:T(8,128)S(1)} %copy-done.1, f32[2560,256]{1,0:T(8,128)S(1)} %copy-done), custom_call_target="tpu_custom_call" | custom-call | tf_op jit(solution)/shard_map/pallas_call | solution.py:359
Async XLA Ops:
  108.9 1.7 %copy-start = (f32[2560,256]{1,0:T(8,128)S(1)}, f32[2560,256]{1,0:T(8,128)}, u32[]{:S(2)}) copy-start(f32[2560,256]{1,0:T(8,128)} %get-tuple-element.5.whole) | copy-start | bytes 7864324
  110.6 1.0 copy-start.1

commit v5 on v4

--- a/solution.py
+++ b/solution.py
@@ -1,4 +1,5 @@
 import functools
+import math
 
 import jax
 import jax.numpy as jnp
@@ -14,6 +15,11 @@
 MESH = pl.DeviceIdType.MESH
 
 
+def plane_of(rows_n):
+    side = math.isqrt(rows_n)
+    return (side, side) if side * side == rows_n else (rows_n, 1)
+
+
 def halves(value):
     top = value.astype(jnp.bfloat16)
     return top, (value - top.astype(jnp.float32)).astype(jnp.bfloat16)
@@ -26,10 +32,10 @@
 
 def body(
     chunk_rows, flags_ref, panel_flags_ref, inv_ref, panel_ref, factor_ref, moved, whole,
-    at_high, at_low, p_high, p_low, l_high, l_low, f_ref, band, partial, got_part, raw,
-    tiles, got_core, sums, got_row, got_line,
+    at_high, at_low, p_high, p_low, l_high, l_low, f_ref, band, partial, part_one, part_mid, part_two, raw,
+    tiles, got_core, sum_one, sum_mid, sum_two, got_row, got_line,
     chain_send, chain_recv, swap_send, swap_recv, part_send, part_recv, move_send, move_recv,
-    sum_send, core_recv, row_recv, line_recv, back_line, back_row, back_core,
+    row_send, row_recv, gather_send, gather_recv, sum_send, core_recv, line_recv, back_line, back_core,
 ):
     rows_n, cols_n = lax.axis_size("row"), lax.axis_size("col")
     line_n = cols_n // 2
@@ -39,9 +45,14 @@
     piece_rows, width = panel_ref.shape
     count = width // TILE
     other_core = (row, 2 * line + 1 - core)
-    row_peers = [((row + d) % rows_n, col) for d in range(1, rows_n)]
+    wide, tall = plane_of(rows_n)
+    px, py = row % wide, row // wide
+    x_at = [(px + d) % wide for d in range(wide)]
+    y_at = [(py + d) % tall for d in range(tall)]
+    x_peers = [(py * wide + x_at[d], col) for d in range(wide)]
+    y_peers = [(y_at[d] * wide + px, col) for d in range(tall)]
     line_peers = [(row, 2 * ((line + d) % line_n) + core) for d in range(1, line_n)]
-    peers = [other_core] + row_peers + line_peers
+    peers = [other_core] + x_peers[1:] + y_peers[1:] + line_peers
     target_at = col * rows_n + row
     target = (target_at // cols_n, target_at % cols_n)
     own_at = row * cols_n + col
@@ -90,6 +101,72 @@
         copy.start()
         return copy
 
+    left, right_half = slice(0, TILE // 2), slice(TILE // 2, TILE)
+
+    def plane_sum(j, view, rows, got_one, middle, got_two, send, recv, n):
+        copies = []
+        for d in range(1, wide):
+            for y in range(tall):
+                slot = d * tall + y
+                src = view(y * wide + x_at[d]).at[:, left]
+                copies.append(begin(src, got_one.at[0, slot, rows], send.at[j, 0, slot], recv.at[j, 0, slot], x_peers[d]))
+        for d in range(1, tall):
+            for x in range(wide):
+                slot = d * wide + x
+                src = view(y_at[d] * wide + x).at[:, right_half]
+                copies.append(begin(src, got_one.at[1, slot, rows], send.at[j, 1, slot], recv.at[j, 1, slot], y_peers[d]))
+        yield "plane", 2 * n, 1.0
+        for copy in copies:
+            copy.wait()
+        for y in range(tall):
+            value = view(y * wide + px)[:, left]
+            for d in range(1, wide):
+                value = value + got_one[0, d * tall + y, rows]
+            middle[0, y, rows] = value
+        for x in range(wide):
+            value = view(py * wide + x)[:, right_half]
+            for d in range(1, tall):
+                value = value + got_one[1, d * wide + x, rows]
+            middle[1, x, rows] = value
+        copies = []
+        for d in range(1, tall):
+            src = middle.at[0, y_at[d], rows]
+            copies.append(begin(src, got_two.at[0, d, rows], send.at[j, 2, d], recv.at[j, 2, d], y_peers[d]))
+        for d in range(1, wide):
+            src = middle.at[1, x_at[d], rows]
+            copies.append(begin(src, got_two.at[1, d, rows], send.at[j, 3, d], recv.at[j, 3, d], x_peers[d]))
+        yield "plane", n, 0.5
+        for copy in copies:
+            copy.wait()
+        one = middle[0, py, rows]
+        for d in range(1, tall):
+            one = one + got_two[0, d, rows]
+        two = middle[1, px, rows]
+        for d in range(1, wide):
+            two = two + got_two[1, d, rows]
+        return jnp.concatenate([one, two], axis=1)
+
+    def plane_gather(j, view, send, recv, n):
+        def share_out(place, half_cols, k, slot, peer):
+            ref = view(place).at[:, half_cols]
+            return begin(ref, ref, send.at[j, k, slot], recv.at[j, k, slot], peer)
+
+        copies = [share_out(row, left, 0, d, x_peers[d]) for d in range(1, wide)]
+        copies += [share_out(row, right_half, 1, d, y_peers[d]) for d in range(1, tall)]
+        yield "plane", n, 0.5
+        for copy in copies:
+            copy.wait()
+        copies = []
+        for d in range(1, tall):
+            for x in range(wide):
+                copies.append(share_out(py * wide + x, left, 2, d * wide + x, y_peers[d]))
+        for d in range(1, wide):
+            for y in range(tall):
+                copies.append(share_out(y * wide + px, right_half, 3, d * tall + y, x_peers[d]))
+        yield "plane", 2 * n, 0.5
+        for copy in copies:
+            copy.wait()
+
     def prepare():
         for a in range(block_rows // TILE):
             for b in range(block_cols // TILE):
@@ -166,18 +243,12 @@
 
         swap(line, 0).wait()
         partial[j] = product((at_high[...], at_low[...]), halves(band[j]), ((1,), (0,)))
-        copies = []
-        for d in range(1, rows_n):
-            to = (row + d) % rows_n
-            src = partial.at[j, span(to * piece_rows, piece_rows)]
-            copies.append(begin(src, got_part.at[j, d], part_send.at[j, d], part_recv.at[j, d], row_peers[d - 1]))
-        yield "plane", 4 * piece_rows * (rows_n - 1) / 3, 3.0
-        for copy in copies:
-            copy.wait()
-        value = partial[j, span(row * piece_rows, piece_rows)]
-        for d in range(1, rows_n):
-            value = value + got_part[j, d]
-        raw[j] = value
+        raw[j] = yield from plane_sum(
+            j,
+            lambda i: partial.at[j, span(i * piece_rows, piece_rows)],
+            slice(j * piece_rows, (j + 1) * piece_rows),
+            part_one, part_mid, part_two, part_send, part_recv, piece_rows,
+        )
         move = lambda: remote(raw.at[j], moved.at[j], move_send.at[j], move_recv.at[j], target)
 
         @pl.when(jnp.logical_not(stays))
@@ -209,34 +280,26 @@
         yield "core", half, 1.0
         copy.wait()
         own = span(base + core * half, half)
-        sums[base_half : base_half + half] = tiles[own] + got_core[base_half : base_half + half]
+        tiles[own] = tiles[own] + got_core[base_half : base_half + half]
         here_part = slice(base_part, base_part + part)
-        copies = []
-        for d in range(1, rows_n):
-            to = (row + d) % rows_n
-            src = sums.at[span(base_half + to * part, part)]
-            copies.append(
-                begin(src, got_row.at[d, here_part], sum_send.at[j, d], row_recv.at[j, d], row_peers[d - 1])
-            )
-        yield "plane", 4 * part, 0.5
-        for copy in copies:
-            copy.wait()
-        value = sums[span(base_half + row * part, part)]
-        for d in range(1, rows_n):
-            value = value + got_row[d, here_part]
-        got_row[0, here_part] = value
+        got_row[here_part] = yield from plane_sum(
+            j,
+            lambda i: tiles.at[span(base + core * half + i * part, part)],
+            here_part,
+            sum_one, sum_mid, sum_two, row_send, row_recv, part,
+        )
         here_piece = slice(base_piece, base_piece + piece)
         copies = []
         for d in range(1, line_n):
             to = (line + d) % line_n
-            src = got_row.at[0, span(base_part + to * piece, piece)]
+            src = got_row.at[span(base_part + to * piece, piece)]
             copies.append(
                 begin(src, got_line.at[d, here_piece], sum_send.at[j, d], line_recv.at[j, d], line_peers[d - 1])
             )
         yield "line", 8 * piece, 0.5
         for copy in copies:
             copy.wait()
-        value = got_row[0, span(base_part + line * piece, piece)]
+        value = got_row[span(base_part + line * piece, piece)]
         for d in range(1, line_n):
             value = value + got_line[d, here_piece]
         mine = span(base + core * half + row * part + line * piece, piece)
@@ -248,14 +311,9 @@
         yield "line", 8 * piece, 0.5
         for copy in copies:
             copy.wait()
-        mine = span(base + core * half + row * part, part)
-        copies = [
-            begin(whole.at[mine], whole.at[mine], sum_send.at[j, d], back_row.at[j, d], row_peers[d - 1])
-            for d in range(1, rows_n)
-        ]
-        yield "plane", 4 * part, 0.5
-        for copy in copies:
-            copy.wait()
+        yield from plane_gather(
+            j, lambda i: whole.at[span(base + core * half + i * part, part)], gather_send, gather_recv, part
+        )
         mine = span(base + core * half, half)
         copy = begin(whole.at[mine], whole.at[mine], sum_send.at[j, 0], back_core.at[j], other_core)
         yield "core", half, 0.5
@@ -308,7 +366,7 @@
     shares = 2 * rows_n * line_n
     chunk_rows = tuple(-(-(count - j) * TILE // (8 * shares)) * 8 * shares for j in range(count))
     total = sum(chunk_rows)
-    most = max(rows_n, line_n)
+    side = max(plane_of(rows_n))
     dma = pltpu.SemaphoreType.DMA
     vmem = pl.BlockSpec(memory_space=pltpu.VMEM)
     smem = pl.BlockSpec(memory_space=pltpu.SMEM)
@@ -331,27 +389,33 @@
             pltpu.VMEM((SHARE, width), f32),
             pltpu.VMEM((count, block_rows, TILE), f32),
             pltpu.VMEM((count, block_cols, TILE), f32),
-            pltpu.VMEM((count, rows_n, piece_rows, TILE), f32),
+            pltpu.VMEM((2, rows_n, count * piece_rows, TILE // 2), f32),
+            pltpu.VMEM((2, side, count * piece_rows, TILE // 2), f32),
+            pltpu.VMEM((2, side, count * piece_rows, TILE // 2), f32),
             pltpu.VMEM((count, piece_rows, TILE), f32),
             pltpu.VMEM((total, TILE), f32),
             pltpu.VMEM((total // 2, TILE), f32),
-            pltpu.VMEM((total // 2, TILE), f32),
-            pltpu.VMEM((rows_n, total // (2 * rows_n), TILE), f32),
+            pltpu.VMEM((2, rows_n, total // (2 * rows_n), TILE // 2), f32),
+            pltpu.VMEM((2, side, total // (2 * rows_n), TILE // 2), f32),
+            pltpu.VMEM((2, side, total // (2 * rows_n), TILE // 2), f32),
+            pltpu.VMEM((total // (2 * rows_n), TILE), f32),
             pltpu.VMEM((line_n, total // shares, TILE), f32),
             dma((count, 2, line_n)),
             dma((count, 2, line_n)),
             dma((count, 2 * line_n)),
             dma((count, 2 * line_n)),
-            dma((count, rows_n)),
-            dma((count, rows_n)),
+            dma((count, 4, rows_n)),
+            dma((count, 4, rows_n)),
             dma((count,)),
             dma((count,)),
-            dma((count, most)),
+            dma((count, 4, rows_n)),
+            dma((count, 4, rows_n)),
+            dma((count, 4, rows_n)),
+            dma((count, 4, rows_n)),
+            dma((count, line_n)),
             dma((count,)),
-            dma((count, rows_n)),
             dma((count, line_n)),
             dma((count, line_n)),
-            dma((count, rows_n)),
             dma((count,)),
         ],
         compiler_params=pltpu.CompilerParams(collective_id=0, has_side_effects=True, vmem_limit_bytes=56 << 20),

time: 115 us -> 125 us (1.087)
  Pallas kernels: 110 us -> 120 us
    pallas_call x1, Pallas kernels: 107 us -> 117 us  [finish(): pl.pallas_call(functools.partial(body, chunk_rows), out_shape=(jax.ShapeD...]
where the time goes in v5:
time: 125 us; the launch traced here: 124 us
  Pallas kernels  120 us (96%)
  local copies, waits for them, and re-layouts  4.13 us (3%)
    pallas_call x1, Pallas kernels, finish(): pl.pallas_call(functools.partial(body, chunk_rows), out_shape=(jax.ShapeD...  117 us
    unnamed x5, local copies, waits for them, and re-layouts  4.13 us
    pallas_call x1, Pallas kernels, finish(): pl.pallas_call(functools.partial(write_out, chunk_rows), grid=(count,), o...  2.83 us

profile of v5, /device:TPU:0, one launch (start us, length us, event | category | flops | bytes accessed | tf_op | source)
XLA Modules:
  0.0 124.4 jit_solution(11807889347530251327)
XLA Ops:
  0.6 1.4 %copy.7.panel_flags_ref = s32[16,4]{1,0:T(8,128)} copy(s32[16,4]{0,1:T(4,128)} %param.9) | data formatting | bytes 512 | tf_op args[4]
  2.0 116.7 %shard_map.68 = (f32[4,128,256]{2,1,0:T(8,128)}, f32[2560,256]{1,0:T(8,128)}) custom-call(s32[16,16]{1,0:T(8,128)} %flags_ref.1, s32[16,4]{1,0:T(8,128)} %copy.7.panel_flags_ref, f32[1024,512]{1,0:T(8,128)} %inv_ref.1, f32[128,1024]{1,0:T(8,128)} %panel_ref.1, f32[1024,1024]{1,0:T(8,128)} %factor_ref.1), custom_call_target="tpu_custom_call" | custom-call | tf_op jit(solution)/shard_map/pallas_call | solution.py:374
  118.7 0.0 copy-start
  118.8 1.7 %copy-done = f32[2560,256]{1,0:T(8,128)S(1)} copy-done((f32[2560,256]{1,0:T(8,128)S(1)}, f32[2560,256]{1,0:T(8,128)}, u32[]{:S(2)}) %copy-start) | copy-done | bytes 2621464
  120.5 0.0 copy-start.1
  120.5 1.0 copy-done.1
  121.5 2.8 %shard_map.69 = (f32[128,1024]{1,0:T(8,128)}, f32[1024,1024]{1,0:T(8,128)}) custom-call(f32[4,128,256]{2,1,0:T(8,128)S(1)} %copy-done.1, f32[2560,256]{1,0:T(8,128)S(1)} %copy-done), custom_call_target="tpu_custom_call" | custom-call | tf_op jit(solution)/shard_map/pallas_call | solution.py:423
Async XLA Ops:
  118.7 1.7 %copy-start = (f32[2560,256]{1,0:T(8,128)S(1)}, f32[2560,256]{1,0:T(8,128)}, u32[]{:S(2)}) copy-start(f32[2560,256]{1,0:T(8,128)} %get-tuple-element.5.whole) | copy-start | bytes 7864324
  120.5 1.0 copy-start.1

commit v6 on v4

--- a/solution.py
+++ b/solution.py
@@ -26,9 +26,9 @@
 
 def body(
     chunk_rows, flags_ref, panel_flags_ref, inv_ref, panel_ref, factor_ref, moved, whole,
-    at_high, at_low, p_high, p_low, l_high, l_low, f_ref, band, partial, got_part, raw,
-    tiles, got_core, sums, got_row, got_line,
-    chain_send, chain_recv, swap_send, swap_recv, part_send, part_recv, move_send, move_recv,
+    at_high, at_low, p_high, p_low, l_high, l_low, f_ref, band, x_there, partial, got_part, raw,
+    tiles, got_core, got_row, got_line, got_full,
+    chain_send, chain_recv, swap_send, swap_recv, part_send, part_recv, move_send, move_recv, ahead_send, ahead_recv,
     sum_send, core_recv, row_recv, line_recv, back_line, back_row, back_core,
 ):
     rows_n, cols_n = lax.axis_size("row"), lax.axis_size("col")
@@ -55,6 +55,7 @@
     @pl.when(jnp.logical_not(stays))
     def _():
         pl.semaphore_signal(barrier, inc=1, device_id=source, device_id_type=MESH)
+        pl.semaphore_signal(barrier, inc=1, device_id=target, device_id_type=MESH)
 
     share = width // (rows_n * cols_n)
     first = own_at * share
@@ -75,7 +76,7 @@
 
     @pl.when(jnp.logical_not(stays))
     def _():
-        pl.semaphore_wait(barrier, len(peers) + 1)
+        pl.semaphore_wait(barrier, len(peers) + 2)
 
     def span(start, size):
         return pl.ds(pl.multiple_of(start, 8), size)
@@ -98,6 +99,10 @@
                 top, rest = halves(tile.T)
                 at_high[b * TILE : (b + 1) * TILE, a * TILE : (a + 1) * TILE] = top
                 at_low[b * TILE : (b + 1) * TILE, a * TILE : (a + 1) * TILE] = rest
+
+    def ahead(j):
+        mine = band.at[j, span(col * piece_rows, piece_rows)]
+        return remote(mine, x_there.at[j], ahead_send.at[j], ahead_recv.at[j], source)
 
     def chunk(j):
         here = slice(j * TILE, (j + 1) * TILE)
@@ -109,7 +114,15 @@
             factor = jnp.concatenate([corner, factor_ref[(j + 1) * TILE :, here]], axis=0)
         scaled = product((p_high[:, j * TILE :], p_low[:, j * TILE :]), halves(factor), ((1,), (0,)))
         band[j, span(col * piece_rows, piece_rows)] = scaled
-        l_high[:, here], l_low[:, here] = halves(jnp.concatenate([scaled, f_ref[:, here]], axis=0))
+
+        @pl.when(jnp.logical_not(stays))
+        def _():
+            ahead(j).start()
+
+        @pl.when(stays)
+        def _():
+            x_there[j] = scaled
+
 
         def piece_of(at, k):
             return band.at[j, span((2 * at + k) * piece_rows, piece_rows)]
@@ -188,16 +201,21 @@
         def _():
             moved[j] = raw[j]
 
-        yield "plane", 2 * piece_rows, 0.5
-
-        @pl.when(jnp.logical_not(stays))
-        def _():
-            move().wait()
-
+        if j == 0:
+            for k in range(count):
+
+                @pl.when(jnp.logical_not(stays))
+                def _():
+                    ahead(k).wait()
+
+                part_here = slice(k * TILE, (k + 1) * TILE)
+                both = jnp.concatenate([x_there[k], f_ref[:, part_here]], axis=0)
+                l_high[:, part_here], l_low[:, part_here] = halves(both)
+        here = slice(j * TILE, (j + 1) * TILE)
         full = (count - j) * TILE
         total = chunk_rows[j]
         base = sum(chunk_rows[:j])
-        right = halves(jnp.concatenate([moved[j], f_ref[:, here]], axis=0))
+        right = halves(jnp.concatenate([raw[j], f_ref[:, here]], axis=0))
         tiles[base : base + full] = product((l_high[:, j * TILE :], l_low[:, j * TILE :]), right, ((0,), (0,)))
         if total > full:
             tiles[base + full : base + total] = jnp.zeros((total - full, TILE), jnp.float32)
@@ -209,45 +227,60 @@
         yield "core", half, 1.0
         copy.wait()
         own = span(base + core * half, half)
-        sums[base_half : base_half + half] = tiles[own] + got_core[base_half : base_half + half]
+        tiles[own] = tiles[own] + got_core[base_half : base_half + half]
         here_part = slice(base_part, base_part + part)
         copies = []
         for d in range(1, rows_n):
             to = (row + d) % rows_n
-            src = sums.at[span(base_half + to * part, part)]
+            src = tiles.at[span(base + core * half + to * part, part)]
             copies.append(
                 begin(src, got_row.at[d, here_part], sum_send.at[j, d], row_recv.at[j, d], row_peers[d - 1])
             )
         yield "plane", 4 * part, 0.5
         for copy in copies:
             copy.wait()
-        value = sums[span(base_half + row * part, part)]
+        value = tiles[span(base + core * half + row * part, part)]
         for d in range(1, rows_n):
             value = value + got_row[d, here_part]
         got_row[0, here_part] = value
-        here_piece = slice(base_piece, base_piece + piece)
-        copies = []
-        for d in range(1, line_n):
-            to = (line + d) % line_n
-            src = got_row.at[0, span(base_part + to * piece, piece)]
-            copies.append(
-                begin(src, got_line.at[d, here_piece], sum_send.at[j, d], line_recv.at[j, d], line_peers[d - 1])
-            )
-        yield "line", 8 * piece, 0.5
-        for copy in copies:
-            copy.wait()
-        value = got_row[0, span(base_part + line * piece, piece)]
-        for d in range(1, line_n):
-            value = value + got_line[d, here_piece]
-        mine = span(base + core * half + row * part + line * piece, piece)
-        whole[mine] = value
-        copies = [
-            begin(whole.at[mine], whole.at[mine], sum_send.at[j, d], back_line.at[j, d], line_peers[d - 1])
-            for d in range(1, line_n)
-        ]
-        yield "line", 8 * piece, 0.5
-        for copy in copies:
-            copy.wait()
+        if j == 0:
+            here_piece = slice(base_piece, base_piece + piece)
+            copies = []
+            for d in range(1, line_n):
+                to = (line + d) % line_n
+                src = got_row.at[0, span(base_part + to * piece, piece)]
+                copies.append(
+                    begin(src, got_line.at[d, here_piece], sum_send.at[j, d], line_recv.at[j, d], line_peers[d - 1])
+                )
+            yield "line", 8 * piece, 0.5
+            for copy in copies:
+                copy.wait()
+            value = got_row[0, span(base_part + line * piece, piece)]
+            for d in range(1, line_n):
+                value = value + got_line[d, here_piece]
+            mine = span(base + core * half + row * part + line * piece, piece)
+            whole[mine] = value
+            copies = [
+                begin(whole.at[mine], whole.at[mine], sum_send.at[j, d], back_line.at[j, d], line_peers[d - 1])
+                for d in range(1, line_n)
+            ]
+            yield "line", 8 * piece, 0.5
+            for copy in copies:
+                copy.wait()
+        else:
+            copies = []
+            for d in range(1, line_n):
+                src = got_row.at[0, here_part]
+                dst = got_full.at[line, here_part]
+                copies.append(begin(src, dst, sum_send.at[j, d], line_recv.at[j, d], line_peers[d - 1]))
+            got_full[line, here_part] = value
+            yield "line", 8 * part, 0.5
+            for copy in copies:
+                copy.wait()
+            value = got_full[0, here_part]
+            for d in range(1, line_n):
+                value = value + got_full[d, here_part]
+            whole[span(base + core * half + row * part, part)] = value
         mine = span(base + core * half + row * part, part)
         copies = [
             begin(whole.at[mine], whole.at[mine], sum_send.at[j, d], back_row.at[j, d], row_peers[d - 1])
@@ -260,6 +293,10 @@
         copy = begin(whole.at[mine], whole.at[mine], sum_send.at[j, 0], back_core.at[j], other_core)
         yield "core", half, 0.5
         copy.wait()
+
+        @pl.when(jnp.logical_not(stays))
+        def _():
+            move().wait()
 
     free = {"line": 0.0, "plane": 0.0, "core": 0.0}
     now = 0.0
@@ -330,20 +367,23 @@
             pltpu.VMEM((piece_rows + SHARE, width), b16),
             pltpu.VMEM((SHARE, width), f32),
             pltpu.VMEM((count, block_rows, TILE), f32),
+            pltpu.VMEM((count, piece_rows, TILE), f32),
             pltpu.VMEM((count, block_cols, TILE), f32),
             pltpu.VMEM((count, rows_n, piece_rows, TILE), f32),
             pltpu.VMEM((count, piece_rows, TILE), f32),
             pltpu.VMEM((total, TILE), f32),
             pltpu.VMEM((total // 2, TILE), f32),
-            pltpu.VMEM((total // 2, TILE), f32),
             pltpu.VMEM((rows_n, total // (2 * rows_n), TILE), f32),
             pltpu.VMEM((line_n, total // shares, TILE), f32),
+            pltpu.VMEM((line_n, total // (2 * rows_n), TILE), f32),
             dma((count, 2, line_n)),
             dma((count, 2, line_n)),
             dma((count, 2 * line_n)),
             dma((count, 2 * line_n)),
             dma((count, rows_n)),
             dma((count, rows_n)),
+            dma((count,)),
+            dma((count,)),
             dma((count,)),
             dma((count,)),
             dma((count, most)),

time: 115 us -> 147 us (1.28)
  Pallas kernels: 110 us -> 142 us
    pallas_call x1, Pallas kernels: 107 us -> 139 us  [finish(): pl.pallas_call(functools.partial(body, chunk_rows), out_shape=(jax.ShapeD...]
where the time goes in v6:
time: 147 us
  Pallas kernels  142 us (97%)
  local copies, waits for them, and re-layouts  4.13 us (3%)
    pallas_call x1, Pallas kernels, finish(): pl.pallas_call(functools.partial(body, chunk_rows), out_shape=(jax.ShapeD...  139 us
    unnamed x5, local copies, waits for them, and re-layouts  4.13 us

profile of v6, /device:TPU:0, one launch (start us, length us, event | category | flops | bytes accessed | tf_op | source)
XLA Modules:
  0.0 146.7 jit_solution(12273310746315312824)
XLA Ops:
  0.6 1.4 copy.7.panel_flags_ref
  2.0 139.1 %shard_map.68 = (f32[4,128,256]{2,1,0:T(8,128)}, f32[2560,256]{1,0:T(8,128)}) custom-call(s32[16,16]{1,0:T(8,128)} %flags_ref.1, s32[16,4]{1,0:T(8,128)} %copy.7.panel_flags_ref, f32[1024,512]{1,0:T(8,128)} %inv_ref.1, f32[128,1024]{1,0:T(8,128)} %panel_ref.1, f32[1024,1024]{1,0:T(8,128)} %factor_ref.1), custom_call_target="tpu_custom_call" | custom-call | tf_op jit(solution)/shard_map/pallas_call | solution.py:353
  141.1 0.0 copy-start
  141.1 1.7 %copy-done = f32[2560,256]{1,0:T(8,128)S(1)} copy-done((f32[2560,256]{1,0:T(8,128)S(1)}, f32[2560,256]{1,0:T(8,128)}, u32[]{:S(2)}) %copy-start) | copy-done | bytes 2621464
  142.8 0.0 copy-start.1
  142.8 1.0 copy-done.1
  143.8 2.8 %shard_map.69 = (f32[128,1024]{1,0:T(8,128)}, f32[1024,1024]{1,0:T(8,128)}) custom-call(f32[4,128,256]{2,1,0:T(8,128)S(1)} %copy-done.1, f32[2560,256]{1,0:T(8,128)S(1)} %copy-done), custom_call_target="tpu_custom_call" | custom-call | tf_op jit(solution)/shard_map/pallas_call | solution.py:399
Async XLA Ops:
  141.1 1.7 %copy-start = (f32[2560,256]{1,0:T(8,128)S(1)}, f32[2560,256]{1,0:T(8,128)}, u32[]{:S(2)}) copy-start(f32[2560,256]{1,0:T(8,128)} %get-tuple-element.5.whole) | copy-start | bytes 7864324
  142.8 1.0 copy-start.1
